TPU v7x, 256 devices: a whole 4x4x8 slice. The times are simulated.
256 devices in a mesh: tm: 8 (over z_lo, core), height: 32 (over x, y, z_hi).
Axes of the slice: x: 4, y: 4, z: 8 (z_hi: 2, z_lo: 4; z = z_hi * 4 + z_lo), core: 2. Of those that a mesh axis runs over, the one named last changes fastest.
Arguments:
- clean_latents: bfloat16 [32, 128, 16, 3072], P('tm', 'height'), may hold values from -6 to 6
- gaussian_noise: bfloat16 [32, 128, 16, 3072], P('tm', 'height'), may hold values from -6 to 6
- text_states: bfloat16 [256, 3072], replicated, may hold values from -6 to 6
- queries: bfloat16 [32, 128, 16, 1536], P('tm', 'height'), may hold values from -40 to 40
- key_states: bfloat16 [32, 128, 16, 1536], P('tm', 'height'), may hold values from -8 to 8
- cotangent: bfloat16 [32, 128, 16, 1536], P('tm', 'height'), may hold values from -240 to 240
- text_keys: bfloat16 [256, 1536], replicated, may hold values from -6 to 6
- window_radii: int32 [12, 3], replicated, may hold values from 0 to 1
- timestep: int32 [1], replicated, may hold values from 200 to 799
- sketch_seed: int32 [1], replicated, may hold values from 0 to 65535
- down_image: bfloat16 [3072, 16], replicated, may hold values from -0.109375 to 0.109375
- up_image: bfloat16 [16, 1536], replicated, may hold values from -1.5 to 1.5
- down_text: bfloat16 [3072, 16], replicated, may hold values from -0.109375 to 0.109375
- up_text: bfloat16 [16, 1536], replicated, may hold values from -1.5 to 1.5
Outputs:
- value_grad: bfloat16 [32, 128, 16, 1536], P('tm', 'height')
- grad_sketch: float32 [16384], replicated
All inputs are finite; a program needn't handle non-finite values.
Results may differ from a plain program's by a relative error of at most 0.0075.
Values may be sent and summed in bfloat16 or wider, within the bound.
A program may use at most 128 MiB of HBM per device.

v0:
```python
import jax
import jax.numpy as jnp
from jax import lax
from jax.sharding import PartitionSpec as P

SKETCH = 16384
TW = 8


def padded_2(block, sides, width):
    for axis, dim in sides:
        count = lax.axis_size(axis)
        forward = [(i, i + 1) for i in range(count - 1)]
        backward = [(target, source) for source, target in forward]
        low = lax.ppermute(
            lax.slice_in_dim(block, block.shape[dim] - width, None, axis=dim), axis, forward
        )
        high = lax.ppermute(lax.slice_in_dim(block, 0, width, axis=dim), axis, backward)
        block = jnp.concatenate([low, block, high], axis=dim)
    return block


def shifted(array, axis, by):
    size = lax.axis_size(axis)
    pairs = [(i, i + by) for i in range(size) if 0 <= i + by < size]
    return lax.ppermute(array, axis, pairs)


def tile_rows(block, width):
    frame_count, row_count, col_count = (block.shape[0], block.shape[1], block.shape[2])
    rest = block.shape[3:]
    col_tiles = col_count // width
    shaped = block.reshape((frame_count, row_count, col_tiles, width) + rest)
    order = (2, 0, 1, 3) + tuple(range(4, 4 + len(rest)))
    return jnp.transpose(shaped, order).reshape((col_tiles, frame_count * row_count * width) + rest)


def region_rows(padded, width):
    col_count = padded.shape[2] - 2 * width
    views = [
        tile_rows(padded[:, :, shift_col * width : shift_col * width + col_count], width)
        for shift_col in range(3)
    ]
    return jnp.concatenate(views, axis=1)


def window_mask(
    radius, frame_tile, row_tile, frame_tiles, row_tiles, col_tiles, frame_count, row_count, width
):
    region = 27 * frame_count * row_count * width
    position = jnp.arange(region, dtype=jnp.int32)
    col_step = position // (9 * frame_count * row_count * width) - 1
    frame_step = position // (3 * row_count * width) % (3 * frame_count) // frame_count - 1
    row_step = position // width % (3 * row_count) // row_count - 1
    inside = (
        (jnp.abs(frame_step) <= radius[0])
        & (jnp.abs(row_step) <= radius[1])
        & (jnp.abs(col_step) <= radius[2])
    )
    inside = inside & (frame_tile + frame_step >= 0) & (frame_tile + frame_step < frame_tiles)
    inside = inside & (row_tile + row_step >= 0) & (row_tile + row_step < row_tiles)
    col_index = jnp.arange(col_tiles, dtype=jnp.int32)[:, None]
    return (
        inside[None, :]
        & (col_index + col_step[None, :] >= 0)
        & (col_index + col_step[None, :] < col_tiles)
    )


def forward_head(query_head, key_region, text_head, cot_head, allowed, score_scale):
    image_scores = (
        jnp.einsum("cqd,cld->cql", query_head, key_region, preferred_element_type=jnp.float32)
        * score_scale
    )
    image_scores = jnp.where(allowed[:, None, :], image_scores, -jnp.inf)
    text_scores = (
        jnp.einsum("cqd,td->cqt", query_head, text_head, preferred_element_type=jnp.float32)
        * score_scale
    )
    row_max = jnp.maximum(jnp.max(image_scores, axis=-1), jnp.max(text_scores, axis=-1))
    total = jnp.sum(jnp.exp(image_scores - row_max[..., None]), axis=-1) + jnp.sum(
        jnp.exp(text_scores - row_max[..., None]), axis=-1
    )
    log_total = row_max + jnp.log(total)
    text_probs = jnp.exp(text_scores - log_total[..., None]).astype(jnp.bfloat16)
    text_part = jnp.einsum("cqt,cqd->td", text_probs, cot_head, preferred_element_type=jnp.float32)
    return (image_scores, log_total, text_part)


def place_back(spread, frame_count, row_count, width):
    col_tiles, head_width = (spread.shape[0], spread.shape[2])
    shaped = spread.reshape(col_tiles, 3, 3 * frame_count, 3 * row_count, width, head_width)
    placed = jnp.zeros((3 * frame_count, 3 * row_count, col_tiles, width, head_width), jnp.float32)
    for shift_col in range(3):
        moved = jnp.transpose(shaped[:, shift_col], (1, 2, 0, 3, 4))
        moved = jnp.pad(moved, ((0, 0), (0, 0), (1, 1), (0, 0), (0, 0)))
        placed = placed + moved[:, :, 2 - shift_col : 2 - shift_col + col_tiles]
    return placed.reshape(3 * frame_count, 3 * row_count, col_tiles * width, head_width)


def sketch_signs(seed_value, rows, width):
    row_part = jnp.arange(rows, dtype=jnp.int32)[:, None] * width
    position = row_part + jnp.arange(width, dtype=jnp.int32)[None, :]
    mixed_bits = position * 1103515245 + seed_value * 12345 + 1013904223
    mixed_bits = mixed_bits ^ mixed_bits >> 16
    mixed_bits = mixed_bits * 73244475
    mixed_bits = mixed_bits ^ mixed_bits >> 16
    return (1 - 2 * (mixed_bits >> 7 & 1)).astype(jnp.float32)


def count_sketch(pieces, seed_value, width, sketch_scale):
    flat = jnp.concatenate([piece.reshape(-1) for piece in pieces]).reshape(-1, width)
    signed = flat * sketch_signs(seed_value, flat.shape[0], width)
    return jnp.sum(signed, axis=0) * sketch_scale


def text_grads(text_hidden, text_value, text_states, up_text):
    highest = lax.Precision.HIGHEST
    text_up_grad = jnp.dot(text_hidden.T, text_value, precision=highest)
    text_back = jnp.dot(text_value, up_text.astype(jnp.float32).T, precision=highest)
    text_down_grad = jnp.dot(text_states.astype(jnp.float32).T, text_back, precision=highest)
    return (text_down_grad, text_up_grad)


def per_device(
    clean_latents,
    gaussian_noise,
    text_states,
    queries,
    key_states,
    cotangent,
    text_keys,
    window_radii,
    timestep,
    sketch_seed,
    down_image,
    up_image,
    down_text,
    up_text,
):
    frame_count, row_count, col_count, value_width = queries.shape
    head_count = window_radii.shape[0]
    head_width = value_width // head_count
    col_tiles = col_count // TW
    score_scale = head_width ** (-0.5)
    frame_tile = lax.axis_index("tm")
    row_tile = lax.axis_index("height")
    frame_tiles = lax.axis_size("tm")
    row_tiles = lax.axis_size("height")
    pad_spec = ((0, 0), (0, 0), (TW, TW), (0, 0))
    key_pad = jnp.pad(padded_2(key_states, (("tm", 0), ("height", 1)), frame_count), pad_spec)
    own_q = tile_rows(queries, TW)
    own_c = tile_rows(cotangent, TW)
    head_ids = jnp.arange(head_count, dtype=jnp.int32)

    def head_mask(head_index):
        return window_mask(
            window_radii[head_index],
            frame_tile,
            row_tile,
            frame_tiles,
            row_tiles,
            col_tiles,
            frame_count,
            row_count,
            TW,
        )

    def forward(head_index):
        offset = head_index * head_width
        allowed = head_mask(head_index)
        query_head = lax.dynamic_slice_in_dim(own_q, offset, head_width, 2)
        cot_head = lax.dynamic_slice_in_dim(own_c, offset, head_width, 2)
        key_region = region_rows(lax.dynamic_slice_in_dim(key_pad, offset, head_width, 3), TW)
        text_head = lax.dynamic_slice_in_dim(text_keys, offset, head_width, 1)
        image_scores, log_total, text_part = forward_head(
            query_head, key_region, text_head, cot_head, allowed, score_scale
        )
        image_probs = jnp.exp(image_scores - log_total[..., None]).astype(jnp.bfloat16)
        spread = jnp.einsum(
            "cql,cqd->cld", image_probs, cot_head, preferred_element_type=jnp.float32
        )
        return (text_part, place_back(spread, frame_count, row_count, TW))

    text_part, head_out = lax.map(forward, head_ids)
    text_value = jnp.transpose(text_part, (1, 0, 2)).reshape(-1, value_width)
    middle = head_out[:, :, row_count : 2 * row_count]
    for direction, border in (
        (-1, head_out[:, :, :row_count]),
        (1, head_out[:, :, 2 * row_count :]),
    ):
        middle = middle + shifted(border.astype(jnp.bfloat16), "height", direction).astype(
            border.dtype
        )
    own_part = middle[:, frame_count : 2 * frame_count]
    for direction, border in ((-1, middle[:, :frame_count]), (1, middle[:, 2 * frame_count :])):
        own_part = own_part + shifted(border.astype(jnp.bfloat16), "tm", direction).astype(
            border.dtype
        )
    value_f32 = jnp.transpose(own_part, (1, 2, 3, 0, 4)).reshape(
        frame_count, row_count, col_count, value_width
    )
    value_grad = value_f32.astype(jnp.bfloat16)
    noise_level = timestep[0].astype(jnp.float32) / 1000.0
    mixed = (
        (1.0 - noise_level) * clean_latents.astype(jnp.float32)
        + noise_level * gaussian_noise.astype(jnp.float32)
    ).astype(jnp.bfloat16)
    mixed = mixed.reshape(-1, mixed.shape[3])
    flat_value = value_grad.reshape(-1, value_width)
    hidden = jnp.dot(mixed, down_image, preferred_element_type=jnp.float32).astype(jnp.bfloat16)
    grad_up = lax.dot_general(
        hidden, flat_value, (((0,), (0,)), ((), ())), preferred_element_type=jnp.float32
    )
    backward_low = lax.dot_general(
        flat_value, up_image, (((1,), (1,)), ((), ())), preferred_element_type=jnp.float32
    ).astype(jnp.bfloat16)
    grad_down = lax.dot_general(
        mixed, backward_low, (((0,), (0,)), ((), ())), preferred_element_type=jnp.float32
    )
    text_hidden = jnp.dot(text_states, down_text, preferred_element_type=jnp.float32)
    token_total = frame_count * row_count * col_count * frame_tiles * row_tiles
    param_total = 2 * grad_down.size + 2 * grad_up.size
    sketch_scale = (token_total * (param_total // SKETCH)) ** (-0.5)
    text_down_grad, text_up_grad = text_grads(text_hidden, text_value, text_states, up_text)
    local_sketch = count_sketch(
        (grad_down, grad_up, text_down_grad, text_up_grad), sketch_seed[0], SKETCH, sketch_scale
    )
    grad_sketch = lax.psum(local_sketch, ("tm", "height"))
    return (value_grad, grad_sketch)


def solution(mesh):
    return jax.shard_map(
        per_device,
        mesh=mesh,
        in_specs=(
            P("tm", "height", None, None),
            P("tm", "height", None, None),
            P(),
            P("tm", "height", None, None),
            P("tm", "height", None, None),
            P("tm", "height", None, None),
            P(),
            P(),
            P(),
            P(),
            P(),
            P(),
            P(),
            P(),
        ),
        out_specs=(P("tm", "height", None, None), P()),
        check_vma=False,
    )
```

profile of v0, /device:TPU:1, one launch (start us, length us, event | category | flops | bytes accessed | tf_op | source)
XLA Modules:
  0.0 920.2 jit_solution(15900157499959258757)
XLA Ops:
  7.2 5.1 collective-permute-start
  12.3 1.9 collective-permute-start.1
  14.2 7.3 collective-permute-done
  22.5 2.1 constant_dynamic-update-slice_fusion.1
  28.1 12.5 %collective-permute-start.2 = (bf16[12,4,16,1536]{3,2,1,0:T(8,128)(2,1)}, bf16[12,4,16,1536]{3,2,1,0:T(8,128)(2,1)}, u32[]{:S(2)}, u32[]{:S(2)}) collective-permute-start(bf16[12,4,16,1536]{3,2,1,0:T(8,128)(2,1)} %constant_dynamic-update-slice_fusion), channel_id=1, source_target_pairs={{0,1},{1,2},{2,3},{3,4},{4,5},{5,6},{6,7},{7,8},{8,9},{9,10},{10,1... | collective-permute-start | bytes 7077896 | tf_op jit(solution)/shard_map/ppermute | solution.py:15
  40.7 2.1 copy.51
  42.8 97.1 %collective-permute-done.3 = bf16[12,4,16,1536]{3,2,1,0:T(8,128)(2,1)} collective-permute-done((bf16[12,4,16,1536]{3,2,1,0:T(8,128)(2,1)}, bf16[12,4,16,1536]{3,2,1,0:T(8,128)(2,1)}, u32[]{:S(2)}, u32[]{:S(2)}) %collective-permute-start.3) | collective-permute-done | bytes 2359328 | tf_op jit(solution)/shard_map/ppermute | solution.py:18
  139.9 9.7 %fusion.52 = bf16[12,12,32,1536]{3,2,1,0:T(8,128)(2,1)} fusion(bf16[12,4,16,1536]{3,2,1,0:T(8,128)(2,1)} %collective-permute-done.3, bf16[12,4,16,1536]{3,2,1,0:T(8,128)(2,1)} %constant_dynamic-update-slice_fusion, bf16[12,4,16,1536]{3,2,1,0:T(8,128)(2,1)} %collective-permute-done.2), kind=kLoop, calls=%fused_computation.99 | loop fusion | flops 84934656 | bytes 21233664 | tf_op jit(solution)/shard_map/concatenate | solution.py:19
  149.6 213.1 %while.15 = (s32[]{:T(128)}, f32[12,256,128]{1,2,0:T(8,128)}, f32[12,12,12,16,128]{4,3,2,1,0:T(8,128)}, s32[12]{0:T(128)S(1)}, bf16[2,128,1536]{2,1,0:T(8,128)(2...) while((s32[]{:T(128)}, f32[12,256,128]{1,2,0:T(8,128)}, ...), condition=%wide.region_5.6_spmd, body=%wide.region_0.5_spmd.sunk | while | flops 499376128 | bytes 40042176 | solution.py:185
  169.7 1.9 dynamic-slice_bitcast_fusion.4
  187.6 2.0 dynamic-slice_bitcast_fusion.4
  193.3 1.9 compare_and_fusion.4
  228.6 1.9 compare_and_fusion.4
  258.5 2.0 dynamic-slice_bitcast_fusion.4
  282.0 1.9 compare_and_fusion.4
  347.4 2.0 dynamic-slice_bitcast_fusion.4
  353.1 1.9 compare_and_fusion.4
  362.7 9.7 %convert.8 = bf16[12,12,12,16,128]{4,3,2,1,0:T(8,128)(2,1)} convert(f32[12,12,12,16,128]{4,3,2,1,0:T(8,128)} %get-tuple-element.191) | non-fusion elementwise | flops 3538944 | bytes 21233664 | tf_op jit(solution)/shard_map/convert.3
  372.4 6.3 fusion.75
  378.7 42.7 %collective-permute-start.5 = (bf16[12,12,4,16,128]{4,3,2,1,0:T(8,128)(2,1)}, bf16[12,12,4,16,128]{4,3,2,1,0:T(8,128)(2,1)}, u32[]{:S(2)}, u32[]{:S(2)}) collective-permute-start(bf16[12,12,4,16,128]{4,3,2,1,0:T(8,128)(2,1)} %get-tuple-element.230), channel_id=1, source_target_pairs={{0,1},{1,2},{2,3},{3,4},{4,5},{5,6},{6,7},{7,8},{8,9},{9,10},{10,1... | collective-permute-start | bytes 7077896 | tf_op jit(solution)/shard_map/ppermute | solution.py:26
  424.5 2.6 add_convert_fusion
  427.1 34.4 %collective-permute-done.5 = bf16[12,12,4,16,128]{4,3,2,1,0:T(8,128)(2,1)} collective-permute-done((bf16[12,12,4,16,128]{4,3,2,1,0:T(8,128)(2,1)}, bf16[12,12,4,16,128]{4,3,2,1,0:T(8,128)(2,1)}, u32[]{:S(2)}, u32[]{:S(2)}) %collective-permute-start.5) | collective-permute-done | bytes 2359328 | tf_op jit(solution)/shard_map/ppermute | solution.py:26
  461.5 108.8 %collective-permute-done.4 = bf16[12,12,4,16,128]{4,3,2,1,0:T(8,128)(2,1)} collective-permute-done((bf16[12,12,4,16,128]{4,3,2,1,0:T(8,128)(2,1)}, bf16[12,12,4,16,128]{4,3,2,1,0:T(8,128)(2,1)}, u32[]{:S(2)}, u32[]{:S(2)}) %collective-permute-start.4) | collective-permute-done | bytes 2359328 | tf_op jit(solution)/shard_map/ppermute | solution.py:26
  570.3 7.4 fusion.71
  579.3 61.7 %collective-permute-start.7 = (bf16[12,4,4,16,128]{4,3,2,1,0:T(8,128)(2,1)}, bf16[12,4,4,16,128]{4,3,2,1,0:T(8,128)(2,1)}, u32[]{:S(2)}, u32[]{:S(2)}) collective-permute-start(bf16[12,4,4,16,128]{4,3,2,1,0:T(8,128)(2,1)} %get-tuple-element.232), channel_id=1, source_target_pairs={{0,32},{32,64},{64,96},{96,128},{128,160},{160,192},{192,224},{1,3... | collective-permute-start | bytes 2359304 | tf_op jit(solution)/shard_map/ppermute | solution.py:26
  641.1 2.1 collective-permute-start.6
  644.6 2.0 fusion.77
  650.9 3.8 collective-permute-done.6
  654.7 2.2 fusion.54
  659.3 2.2 fusion.55
  662.2 3.7 fusion.56
  672.2 239.7 %all-reduce.5.cloned.1.call-done = f32[16384]{0:T(1024)} async-done(((f32[16384]{0:T(1024)}), f32[16384]{0:T(1024)}) %all-reduce.5.cloned.1.call-update) | async-done | bytes 65552 | tf_op jit(solution)/shard_map/psum | solution.py:229
  (328 shorter events, 190.9 us)
Async XLA Ops:
  7.2 416.8 %copy-start = (bf16[256,3072]{1,0:T(8,128)(2,1)S(1)}, bf16[256,3072]{1,0:T(8,128)(2,1)}, u32[]{:S(2)}) copy-start(bf16[256,3072]{1,0:T(8,128)(2,1)} %param.18) | copy-start | bytes 4718596
  7.2 33.5 %copy-start.6 = (bf16[4,4,16,1536]{3,2,1,0:T(8,128)(2,1)S(1)}, bf16[4,4,16,1536]{3,2,1,0:T(8,128)(2,1)}, u32[]{:S(2)}) copy-start(bf16[4,4,16,1536]{3,2,1,0:T(8,128)(2,1)} %param.19) | copy-start | bytes 2359300
  7.2 904.7 %all-reduce.5.cloned.1.call-start = ((), (), s32[]{:S(2)}) async-start(), calls=%async_computation | async-start | bytes 131072 | tf_op jit(solution)/shard_map/psum | solution.py:229
  7.2 14.3 %collective-permute-start = (bf16[4,4,16,1536]{3,2,1,0:T(8,128)(2,1)}, bf16[4,4,16,1536]{3,2,1,0:T(8,128)(2,1)S(1)}, u32[]{:S(2)}, u32[]{:S(2)}) collective-permute-start(bf16[4,4,16,1536]{3,2,1,0:T(8,128)(2,1)} %param.20), channel_id=1, source_target_pairs={{0,32},{32,64},{64,96},{96,128},{128,160},{160,192},{192,224},{1,3... | collective-permute-start | bytes 2359304 | tf_op jit(solution)/shard_map/ppermute | solution.py:15
  12.3 13.5 %collective-permute-start.1 = (bf16[4,4,16,1536]{3,2,1,0:T(8,128)(2,1)}, bf16[4,4,16,1536]{3,2,1,0:T(8,128)(2,1)S(1)}, u32[]{:S(2)}, u32[]{:S(2)}) collective-permute-start(bf16[4,4,16,1536]{3,2,1,0:T(8,128)(2,1)} %param.20), channel_id=1, source_target_pairs={{32,0},{64,32},{96,64},{128,96},{160,128},{192,160},{224,192},{33,... | collective-permute-start | bytes 2359304 | tf_op jit(solution)/shard_map/ppermute | solution.py:18
  26.8 113.1 %collective-permute-start.3 = (bf16[12,4,16,1536]{3,2,1,0:T(8,128)(2,1)}, bf16[12,4,16,1536]{3,2,1,0:T(8,128)(2,1)}, u32[]{:S(2)}, u32[]{:S(2)}) collective-permute-start(bf16[12,4,16,1536]{3,2,1,0:T(8,128)(2,1)} %constant_dynamic-update-slice_fusion), channel_id=1, source_target_pairs={{1,0},{2,1},{3,2},{4,3},{5,4},{6,5},{7,6},{8,7},{9,8},{10,9},{11,1... | collective-permute-start | bytes 7077896 | tf_op jit(solution)/shard_map/ppermute | solution.py:18
  28.1 111.8 %collective-permute-start.2 = (bf16[12,4,16,1536]{3,2,1,0:T(8,128)(2,1)}, bf16[12,4,16,1536]{3,2,1,0:T(8,128)(2,1)}, u32[]{:S(2)}, u32[]{:S(2)}) collective-permute-start(bf16[12,4,16,1536]{3,2,1,0:T(8,128)(2,1)} %constant_dynamic-update-slice_fusion), channel_id=1, source_target_pairs={{0,1},{1,2},{2,3},{3,4},{4,5},{5,6},{6,7},{7,8},{8,9},{9,10},{10,1... | collective-permute-start | bytes 7077896 | tf_op jit(solution)/shard_map/ppermute | solution.py:15
  42.8 106.8 %copy-start.9 = (s32[12,3]{0,1:T(4,128)S(1)}, s32[12,3]{0,1:T(4,128)}, u32[]{:S(2)}) copy-start(s32[12,3]{0,1:T(4,128)} %param.23) | copy-start | bytes 436
  149.6 4.3 copy-start.4
  167.3 4.4 copy-start.4
  183.8 1.2 copy-start.5
  185.1 4.5 copy-start.4
  202.9 4.3 copy-start.4
  220.6 4.3 copy-start.4
  238.3 4.3 copy-start.4
  256.1 4.5 copy-start.4
  272.7 1.2 copy-start.5
  273.9 4.3 copy-start.4
  291.6 4.3 copy-start.4
  309.3 4.4 copy-start.4
  325.9 1.3 copy-start.5
  327.1 4.4 copy-start.4
  344.9 4.4 copy-start.4
  372.4 51.6 %copy-start.8 = (bf16[3072,16]{0,1:T(8,128)(2,1)S(1)}, bf16[3072,16]{0,1:T(8,128)(2,1)}, u32[]{:S(2)}) copy-start(bf16[3072,16]{0,1:T(8,128)(2,1)} %param.28) | copy-start | bytes 294916
  378.7 82.8 %collective-permute-start.5 = (bf16[12,12,4,16,128]{4,3,2,1,0:T(8,128)(2,1)}, bf16[12,12,4,16,128]{4,3,2,1,0:T(8,128)(2,1)}, u32[]{:S(2)}, u32[]{:S(2)}) collective-permute-start(bf16[12,12,4,16,128]{4,3,2,1,0:T(8,128)(2,1)} %get-tuple-element.230), channel_id=1, source_target_pairs={{0,1},{1,2},{2,3},{3,4},{4,5},{5,6},{6,7},{7,8},{8,9},{9,10},{10,1... | collective-permute-start | bytes 7077896 | tf_op jit(solution)/shard_map/ppermute | solution.py:26
  421.4 148.9 %collective-permute-start.4 = (bf16[12,12,4,16,128]{4,3,2,1,0:T(8,128)(2,1)}, bf16[12,12,4,16,128]{4,3,2,1,0:T(8,128)(2,1)}, u32[]{:S(2)}, u32[]{:S(2)}) collective-permute-start(bf16[12,12,4,16,128]{4,3,2,1,0:T(8,128)(2,1)} %get-tuple-element.229), channel_id=1, source_target_pairs={{1,0},{2,1},{3,2},{4,3},{5,4},{6,5},{7,6},{8,7},{9,8},{10,9},{11,1... | collective-permute-start | bytes 7077896 | tf_op jit(solution)/shard_map/ppermute | solution.py:26
  577.7 65.5 %copy-start.3 = (f32[12,256,128]{1,2,0:T(8,128)S(1)}, f32[12,256,128]{1,2,0:T(8,128)}, u32[]{:S(2)}) copy-start(f32[12,256,128]{1,2,0:T(8,128)} %get-tuple-element.192) | copy-start | bytes 4718596
  577.7 66.9 %copy-start.10 = (bf16[16,1536]{1,0:T(8,128)(2,1)S(1)}, bf16[16,1536]{1,0:T(8,128)(2,1)}, u32[]{:S(2)}) copy-start(bf16[16,1536]{1,0:T(8,128)(2,1)} %param.29) | copy-start | bytes 147460
  579.3 71.6 %collective-permute-start.7 = (bf16[12,4,4,16,128]{4,3,2,1,0:T(8,128)(2,1)}, bf16[12,4,4,16,128]{4,3,2,1,0:T(8,128)(2,1)}, u32[]{:S(2)}, u32[]{:S(2)}) collective-permute-start(bf16[12,4,4,16,128]{4,3,2,1,0:T(8,128)(2,1)} %get-tuple-element.232), channel_id=1, source_target_pairs={{0,32},{32,64},{64,96},{96,128},{128,160},{160,192},{192,224},{1,3... | collective-permute-start | bytes 2359304 | tf_op jit(solution)/shard_map/ppermute | solution.py:26
  641.1 13.6 %collective-permute-start.6 = (bf16[12,4,4,16,128]{4,3,2,1,0:T(8,128)(2,1)}, bf16[12,4,4,16,128]{4,3,2,1,0:T(8,128)(2,1)}, u32[]{:S(2)}, u32[]{:S(2)}) collective-permute-start(bf16[12,4,4,16,128]{4,3,2,1,0:T(8,128)(2,1)} %get-tuple-element.231), channel_id=1, source_target_pairs={{32,0},{64,32},{96,64},{128,96},{160,128},{192,160},{224,192},{33,... | collective-permute-start | bytes 2359304 | tf_op jit(solution)/shard_map/ppermute | solution.py:26
  662.2 5.5 copy-start.7
  667.7 3.5 copy-start.2
  (10 other events, 11.9 us)
Sparse Core Ops, SparseCore 0:
  671.3 240.5 all-reduce.4
where the time goes:
time: 925 us; the launch traced here: 920 us
  waiting for transfers between devices  492 us (53%)
  starting transfers between devices  129 us (14%)
  matrix products  89.3 us (10%)
  other arithmetic  82 us (9%)
  local copies, waits for them, and re-layouts  81.4 us (9%)
  loops' own time  31 us (3%)
  between operations  15.5 us (2%)
    psum x1, waiting for transfers between devices, per_device(): grad_sketch = lax.psum(local_sketch, ('tm', 'height'))  240 us
    ppermute x4, waiting for transfers between devices, shifted(): return lax.ppermute(array, axis, pairs)  147 us
    ppermute x4, starting transfers between devices, shifted(): return lax.ppermute(array, axis, pairs)  108 us
    ppermute x2, waiting for transfers between devices, padded_2(): lax.ppermute(lax.slice_in_dim(block, 0, width, axis=dim), axis, backward)  98.3 us
    reshape x50, local copies, waits for them, and re-layouts, tile_rows(): shaped = block.reshape((frame_count, row_count, col_tiles, width) + rest)  38.7 us
    another operation x1, loops' own time, per_device(): text_part, head_out = lax.map(forward, head_ids)  31 us
    and x12, other arithmetic, window_mask(): inside & (row_tile + row_step >= 0) & (row_tile + row_step < row_tiles)  23 us
    dot_general x12, matrix products, forward(): jnp.einsum('cql,cqd->cld', image_probs, cot_head, preferred_element_type=...  22.2 us
  transfers between devices with their start and end apart: 9, of which 7 were waited for; matrix products, arithmetic and copies ran while one was open for 2% of the time, Pallas kernels for 0%

commit v1 on v0

--- a/solution.py
+++ b/solution.py
@@ -226,7 +226,7 @@
     local_sketch = count_sketch(
         (grad_down, grad_up, text_down_grad, text_up_grad), sketch_seed[0], SKETCH, sketch_scale
     )
-    grad_sketch = lax.psum(local_sketch, ("tm", "height"))
+    grad_sketch = lax.psum(lax.psum(local_sketch, "height"), "tm")
     return (value_grad, grad_sketch)
 
 

time: 925 us -> 1150 us (1.24)
  waiting for transfers between devices: 492 us -> 716 us
    psum x1 -> x2, waiting for transfers between devices: 240 us -> 463 us  [per_device(): grad_sketch = lax.psum(lax.psum(local_sketch, 'height'), 'tm')]
  transfers between devices with their start and end apart: 9 -> 10, of which waited for: 7 -> 8; matrix products, arithmetic and copies ran while one was open for 2% -> 1% of each run, Pallas kernels for 0% -> 0%
where the time goes in v1:
time: 1150 us; the launch traced here: 1140 us
  waiting for transfers between devices  716 us (62%)
  starting transfers between devices  129 us (11%)
  matrix products  89.3 us (8%)
  other arithmetic  82 us (7%)
  local copies, waits for them, and re-layouts  81.4 us (7%)
  loops' own time  31 us (3%)
  between operations  15.6 us (1%)
    psum x2, waiting for transfers between devices, per_device(): grad_sketch = lax.psum(lax.psum(local_sketch, 'height'), 'tm')  463 us
    ppermute x4, waiting for transfers between devices, shifted(): return lax.ppermute(array, axis, pairs)  147 us
    ppermute x4, starting transfers between devices, shifted(): return lax.ppermute(array, axis, pairs)  108 us
    ppermute x2, waiting for transfers between devices, padded_2(): lax.ppermute(lax.slice_in_dim(block, 0, width, axis=dim), axis, backward)  98.3 us
    reshape x50, local copies, waits for them, and re-layouts, tile_rows(): shaped = block.reshape((frame_count, row_count, col_tiles, width) + rest)  38.7 us
    another operation x1, loops' own time, per_device(): text_part, head_out = lax.map(forward, head_ids)  31 us
    and x12, other arithmetic, window_mask(): inside & (row_tile + row_step >= 0) & (row_tile + row_step < row_tiles)  23 us
  transfers between devices with their start and end apart: 10, of which 8 were waited for; matrix products, arithmetic and copies ran while one was open for 1% of the time, Pallas kernels for 0%

profile of v1, /device:TPU:1, one launch (start us, length us, event | category | flops | bytes accessed | tf_op | source)
XLA Modules:
  0.0 1143.8 jit_solution(15439428069263182074)
XLA Ops:
  7.2 5.1 collective-permute-start
  12.3 1.9 collective-permute-start.1
  14.2 7.3 collective-permute-done
  22.5 2.1 constant_dynamic-update-slice_fusion.1
  28.1 12.5 %collective-permute-start.2 = (bf16[12,4,16,1536]{3,2,1,0:T(8,128)(2,1)}, bf16[12,4,16,1536]{3,2,1,0:T(8,128)(2,1)}, u32[]{:S(2)}, u32[]{:S(2)}) collective-permute-start(bf16[12,4,16,1536]{3,2,1,0:T(8,128)(2,1)} %constant_dynamic-update-slice_fusion), channel_id=1, source_target_pairs={{0,1},{1,2},{2,3},{3,4},{4,5},{5,6},{6,7},{7,8},{8,9},{9,10},{10,1... | collective-permute-start | bytes 7077896 | tf_op jit(solution)/shard_map/ppermute | solution.py:15
  40.7 2.1 copy.51
  42.8 97.1 %collective-permute-done.3 = bf16[12,4,16,1536]{3,2,1,0:T(8,128)(2,1)} collective-permute-done((bf16[12,4,16,1536]{3,2,1,0:T(8,128)(2,1)}, bf16[12,4,16,1536]{3,2,1,0:T(8,128)(2,1)}, u32[]{:S(2)}, u32[]{:S(2)}) %collective-permute-start.3) | collective-permute-done | bytes 2359328 | tf_op jit(solution)/shard_map/ppermute | solution.py:18
  139.9 9.7 fusion.52
  149.6 213.1 %while.15 = (s32[]{:T(128)}, f32[12,256,128]{1,2,0:T(8,128)}, f32[12,12,12,16,128]{4,3,2,1,0:T(8,128)}, s32[12]{0:T(128)S(1)}, bf16[2,128,1536]{2,1,0:T(8,128)(2...) while((s32[]{:T(128)}, f32[12,256,128]{1,2,0:T(8,128)}, ...), condition=%wide.region_5.6_spmd, body=%wide.region_0.5_spmd.sunk | while | flops 499376128 | bytes 40042176 | solution.py:185
  169.7 1.9 dynamic-slice_bitcast_fusion.4
  187.6 2.0 dynamic-slice_bitcast_fusion.4
  193.3 1.9 compare_and_fusion.4
  228.6 1.9 compare_and_fusion.4
  258.5 2.0 dynamic-slice_bitcast_fusion.4
  282.0 1.9 compare_and_fusion.4
  347.4 2.0 dynamic-slice_bitcast_fusion.4
  362.7 9.7 convert.8
  372.4 6.3 fusion.75
  378.7 42.7 %collective-permute-start.5 = (bf16[12,12,4,16,128]{4,3,2,1,0:T(8,128)(2,1)}, bf16[12,12,4,16,128]{4,3,2,1,0:T(8,128)(2,1)}, u32[]{:S(2)}, u32[]{:S(2)}) collective-permute-start(bf16[12,12,4,16,128]{4,3,2,1,0:T(8,128)(2,1)} %get-tuple-element.230), channel_id=1, source_target_pairs={{0,1},{1,2},{2,3},{3,4},{4,5},{5,6},{6,7},{7,8},{8,9},{9,10},{10,1... | collective-permute-start | bytes 7077896 | tf_op jit(solution)/shard_map/ppermute | solution.py:26
  424.5 2.6 add_convert_fusion
  427.1 34.4 %collective-permute-done.5 = bf16[12,12,4,16,128]{4,3,2,1,0:T(8,128)(2,1)} collective-permute-done((bf16[12,12,4,16,128]{4,3,2,1,0:T(8,128)(2,1)}, bf16[12,12,4,16,128]{4,3,2,1,0:T(8,128)(2,1)}, u32[]{:S(2)}, u32[]{:S(2)}) %collective-permute-start.5) | collective-permute-done | bytes 2359328 | tf_op jit(solution)/shard_map/ppermute | solution.py:26
  461.5 108.8 %collective-permute-done.4 = bf16[12,12,4,16,128]{4,3,2,1,0:T(8,128)(2,1)} collective-permute-done((bf16[12,12,4,16,128]{4,3,2,1,0:T(8,128)(2,1)}, bf16[12,12,4,16,128]{4,3,2,1,0:T(8,128)(2,1)}, u32[]{:S(2)}, u32[]{:S(2)}) %collective-permute-start.4) | collective-permute-done | bytes 2359328 | tf_op jit(solution)/shard_map/ppermute | solution.py:26
  570.3 7.4 fusion.71
  579.3 61.7 %collective-permute-start.7 = (bf16[12,4,4,16,128]{4,3,2,1,0:T(8,128)(2,1)}, bf16[12,4,4,16,128]{4,3,2,1,0:T(8,128)(2,1)}, u32[]{:S(2)}, u32[]{:S(2)}) collective-permute-start(bf16[12,4,4,16,128]{4,3,2,1,0:T(8,128)(2,1)} %get-tuple-element.232), channel_id=1, source_target_pairs={{0,32},{32,64},{64,96},{96,128},{128,160},{160,192},{192,224},{1,3... | collective-permute-start | bytes 2359304 | tf_op jit(solution)/shard_map/ppermute | solution.py:26
  641.1 2.1 collective-permute-start.6
  644.6 2.0 fusion.77
  650.9 3.8 collective-permute-done.6
  654.7 2.2 fusion.54
  659.3 2.2 fusion.55
  662.2 3.7 fusion.56
  671.2 377.6 %all-reduce.6.cloned.1.call-done = f32[16384]{0:T(1024)} async-done(((f32[16384]{0:T(1024)}), f32[16384]{0:T(1024)}) %all-reduce.6.cloned.1.call-update) | async-done | bytes 65552 | tf_op jit(solution)/shard_map/psum | solution.py:229
  1049.8 85.6 %all-reduce.8.cloned.1.call-done = f32[16384]{0:T(1024)} async-done(((f32[16384]{0:T(1024)}), f32[16384]{0:T(1024)}) %all-reduce.8.cloned.1.call-update) | async-done | bytes 65552 | tf_op jit(solution)/shard_map/psum | solution.py:229
  (331 shorter events, 192.9 us)
Async XLA Ops:
  7.2 416.8 %copy-start = (bf16[256,3072]{1,0:T(8,128)(2,1)S(1)}, bf16[256,3072]{1,0:T(8,128)(2,1)}, u32[]{:S(2)}) copy-start(bf16[256,3072]{1,0:T(8,128)(2,1)} %param.18) | copy-start | bytes 4718596
  7.2 33.5 %copy-start.6 = (bf16[4,4,16,1536]{3,2,1,0:T(8,128)(2,1)S(1)}, bf16[4,4,16,1536]{3,2,1,0:T(8,128)(2,1)}, u32[]{:S(2)}) copy-start(bf16[4,4,16,1536]{3,2,1,0:T(8,128)(2,1)} %param.19) | copy-start | bytes 2359300
  7.2 1041.6 %all-reduce.6.cloned.1.call-start = ((), (), s32[]{:S(2)}) async-start(), calls=%async_computation | async-start | bytes 131072 | tf_op jit(solution)/shard_map/psum | solution.py:229
  7.2 14.3 %collective-permute-start = (bf16[4,4,16,1536]{3,2,1,0:T(8,128)(2,1)}, bf16[4,4,16,1536]{3,2,1,0:T(8,128)(2,1)S(1)}, u32[]{:S(2)}, u32[]{:S(2)}) collective-permute-start(bf16[4,4,16,1536]{3,2,1,0:T(8,128)(2,1)} %param.20), channel_id=1, source_target_pairs={{0,32},{32,64},{64,96},{96,128},{128,160},{160,192},{192,224},{1,3... | collective-permute-start | bytes 2359304 | tf_op jit(solution)/shard_map/ppermute | solution.py:15
  12.3 13.5 %collective-permute-start.1 = (bf16[4,4,16,1536]{3,2,1,0:T(8,128)(2,1)}, bf16[4,4,16,1536]{3,2,1,0:T(8,128)(2,1)S(1)}, u32[]{:S(2)}, u32[]{:S(2)}) collective-permute-start(bf16[4,4,16,1536]{3,2,1,0:T(8,128)(2,1)} %param.20), channel_id=1, source_target_pairs={{32,0},{64,32},{96,64},{128,96},{160,128},{192,160},{224,192},{33,... | collective-permute-start | bytes 2359304 | tf_op jit(solution)/shard_map/ppermute | solution.py:18
  26.8 113.1 %collective-permute-start.3 = (bf16[12,4,16,1536]{3,2,1,0:T(8,128)(2,1)}, bf16[12,4,16,1536]{3,2,1,0:T(8,128)(2,1)}, u32[]{:S(2)}, u32[]{:S(2)}) collective-permute-start(bf16[12,4,16,1536]{3,2,1,0:T(8,128)(2,1)} %constant_dynamic-update-slice_fusion), channel_id=1, source_target_pairs={{1,0},{2,1},{3,2},{4,3},{5,4},{6,5},{7,6},{8,7},{9,8},{10,9},{11,1... | collective-permute-start | bytes 7077896 | tf_op jit(solution)/shard_map/ppermute | solution.py:18
  28.1 111.8 %collective-permute-start.2 = (bf16[12,4,16,1536]{3,2,1,0:T(8,128)(2,1)}, bf16[12,4,16,1536]{3,2,1,0:T(8,128)(2,1)}, u32[]{:S(2)}, u32[]{:S(2)}) collective-permute-start(bf16[12,4,16,1536]{3,2,1,0:T(8,128)(2,1)} %constant_dynamic-update-slice_fusion), channel_id=1, source_target_pairs={{0,1},{1,2},{2,3},{3,4},{4,5},{5,6},{6,7},{7,8},{8,9},{9,10},{10,1... | collective-permute-start | bytes 7077896 | tf_op jit(solution)/shard_map/ppermute | solution.py:15
  42.8 106.8 %copy-start.9 = (s32[12,3]{0,1:T(4,128)S(1)}, s32[12,3]{0,1:T(4,128)}, u32[]{:S(2)}) copy-start(s32[12,3]{0,1:T(4,128)} %param.23) | copy-start | bytes 436
  149.6 4.3 copy-start.4
  167.3 4.4 copy-start.4
  185.1 4.5 copy-start.4
  202.9 4.3 copy-start.4
  220.6 4.3 copy-start.4
  238.3 4.3 copy-start.4
  256.1 4.5 copy-start.4
  272.7 1.2 copy-start.5
  273.9 4.3 copy-start.4
  291.6 4.3 copy-start.4
  309.3 4.4 copy-start.4
  325.9 1.3 copy-start.5
  327.1 4.4 copy-start.4
  344.9 4.4 copy-start.4
  372.4 51.6 %copy-start.8 = (bf16[3072,16]{0,1:T(8,128)(2,1)S(1)}, bf16[3072,16]{0,1:T(8,128)(2,1)}, u32[]{:S(2)}) copy-start(bf16[3072,16]{0,1:T(8,128)(2,1)} %param.28) | copy-start | bytes 294916
  378.7 82.8 %collective-permute-start.5 = (bf16[12,12,4,16,128]{4,3,2,1,0:T(8,128)(2,1)}, bf16[12,12,4,16,128]{4,3,2,1,0:T(8,128)(2,1)}, u32[]{:S(2)}, u32[]{:S(2)}) collective-permute-start(bf16[12,12,4,16,128]{4,3,2,1,0:T(8,128)(2,1)} %get-tuple-element.230), channel_id=1, source_target_pairs={{0,1},{1,2},{2,3},{3,4},{4,5},{5,6},{6,7},{7,8},{8,9},{9,10},{10,1... | collective-permute-start | bytes 7077896 | tf_op jit(solution)/shard_map/ppermute | solution.py:26
  421.4 148.9 %collective-permute-start.4 = (bf16[12,12,4,16,128]{4,3,2,1,0:T(8,128)(2,1)}, bf16[12,12,4,16,128]{4,3,2,1,0:T(8,128)(2,1)}, u32[]{:S(2)}, u32[]{:S(2)}) collective-permute-start(bf16[12,12,4,16,128]{4,3,2,1,0:T(8,128)(2,1)} %get-tuple-element.229), channel_id=1, source_target_pairs={{1,0},{2,1},{3,2},{4,3},{5,4},{6,5},{7,6},{8,7},{9,8},{10,9},{11,1... | collective-permute-start | bytes 7077896 | tf_op jit(solution)/shard_map/ppermute | solution.py:26
  577.7 65.5 %copy-start.3 = (f32[12,256,128]{1,2,0:T(8,128)S(1)}, f32[12,256,128]{1,2,0:T(8,128)}, u32[]{:S(2)}) copy-start(f32[12,256,128]{1,2,0:T(8,128)} %get-tuple-element.192) | copy-start | bytes 4718596
  577.7 66.9 %copy-start.10 = (bf16[16,1536]{1,0:T(8,128)(2,1)S(1)}, bf16[16,1536]{1,0:T(8,128)(2,1)}, u32[]{:S(2)}) copy-start(bf16[16,1536]{1,0:T(8,128)(2,1)} %param.29) | copy-start | bytes 147460
  579.3 71.6 %collective-permute-start.7 = (bf16[12,4,4,16,128]{4,3,2,1,0:T(8,128)(2,1)}, bf16[12,4,4,16,128]{4,3,2,1,0:T(8,128)(2,1)}, u32[]{:S(2)}, u32[]{:S(2)}) collective-permute-start(bf16[12,4,4,16,128]{4,3,2,1,0:T(8,128)(2,1)} %get-tuple-element.232), channel_id=1, source_target_pairs={{0,32},{32,64},{64,96},{96,128},{128,160},{160,192},{192,224},{1,3... | collective-permute-start | bytes 2359304 | tf_op jit(solution)/shard_map/ppermute | solution.py:26
  641.1 13.6 %collective-permute-start.6 = (bf16[12,4,4,16,128]{4,3,2,1,0:T(8,128)(2,1)}, bf16[12,4,4,16,128]{4,3,2,1,0:T(8,128)(2,1)}, u32[]{:S(2)}, u32[]{:S(2)}) collective-permute-start(bf16[12,4,4,16,128]{4,3,2,1,0:T(8,128)(2,1)} %get-tuple-element.231), channel_id=1, source_target_pairs={{32,0},{64,32},{96,64},{128,96},{160,128},{192,160},{224,192},{33,... | collective-permute-start | bytes 2359304 | tf_op jit(solution)/shard_map/ppermute | solution.py:26
  662.2 5.5 copy-start.7
  667.7 381.1 %copy-start.2 = (bf16[12,4,4,16,128]{4,3,2,1,0:T(8,128)(2,1)S(1)}, bf16[12,4,4,16,128]{4,3,2,1,0:T(8,128)(2,1)}, u32[]{:S(2)}) copy-start(bf16[12,4,4,16,128]{4,3,2,1,0:T(8,128)(2,1)} %copy-done.1) | copy-start | bytes 2359300
  671.2 464.3 %all-reduce.8.cloned.1.call-start = ((), (), s32[]{:S(2)}) async-start(), calls=%async_computation.1 | async-start | bytes 131072 | tf_op jit(solution)/shard_map/psum | solution.py:229
  (11 other events, 13.2 us)
Sparse Core Ops, SparseCore 0:
  671.3 377.4 all-reduce.5
  1051.6 83.8 all-reduce.7
